TPU v7x, 128 devices: a whole 4x4x4 slice. The times are simulated.
128 devices in a mesh: kv: 32 (over y, x, core), head: 4 (over z).
Axes of the slice: x: 4, y: 4, z: 4, core: 2. Of those that a mesh axis runs over, the one named last changes fastest.
Arguments:
- queries: bfloat16 [8, 16384], P(None, 'head'), may hold values from -9 to 9
- kv_cache: bfloat16 [8, 16384, 2, 1024], P(None, 'kv', None, 'head'), may hold values from -12 to 12
- new_kv: bfloat16 [8, 2, 1024], P(None, None, 'head'), may hold values from -12 to 12
- offsets: int32 [8], replicated, may hold values from 0 to 31, as said below
- lengths: int32 [8], replicated, may hold values from 4096 to 16384, as said below
- residual: bfloat16 [8, 16384], P(None, ('kv', 'head')), may hold values from -6 to 6
- out_weight: bfloat16 [16384, 16384], P('head', 'kv'), may hold values from -0.046875 to 0.046875
- norm_gain: bfloat16 [16384], P(('kv', 'head')), may hold values from 0.099609375 to 1.8984375
- gate_weight: bfloat16 [16384, 32768], P(None, ('kv', 'head')), may hold values from -0.046875 to 0.046875
- up_weight: bfloat16 [16384, 32768], P(None, ('kv', 'head')), may hold values from -0.046875 to 0.046875
Outputs:
- stream: bfloat16 [8, 16384], P(None, ('kv', 'head'))
- gated: bfloat16 [8, 32768], P(None, ('kv', 'head'))
Inputs may be any that keep to these rules, and one draw needn't show every extreme that they name: Position p of sequence b sits on kv index (offsets[b] + p // 512) mod 32, slot p mod 512 there. `lengths`: in every draw some sequence fills all 16384 slots.
All inputs are finite; a program needn't handle non-finite values.
Results may differ from a plain program's by a relative error of at most 0.04.
Values may be sent and summed in bfloat16 or wider, within the bound.
No kernel may reach another device: no remote copies, remote signals or barrier semaphores. Data moves between devices by JAX's collectives and lax.ppermute only.
A program may use at most 128 MiB of HBM per device.

v0:
```python
import jax
import jax.numpy as jnp
from jax import lax
from jax.experimental import pallas as pl
from jax.experimental.pallas import tpu as pltpu
from jax.sharding import Mesh
from jax.sharding import PartitionSpec as P

D = 16384
HD = 128
HALF = HD // 2
F32 = jnp.float32
BF16 = jnp.bfloat16
LOG2E = 1.4426950408889634
VMEM = pl.BlockSpec(memory_space=pltpu.VMEM)
HBM = pl.BlockSpec(memory_space=pltpu.HBM)
MIB = 1 << 20
KV = ("y", "x", "core")
ALL = ("y", "x", "core", "head")


def lanes(rows):
    return lax.broadcasted_iota(jnp.int32, (rows, HD), 1)


def attention_kernel(
    offs_hbm, lens_hbm, q_hbm, new_hbm, cache, out_ref, offs, lens, q_ref, new_ref, buf, q_by_row, sems
):
    rows, width, _ = cache.shape
    heads = q_ref.shape[1] // HD
    group = heads // 2
    slots = width // 4
    small = [
        pltpu.make_async_copy(source, target, sems.at[rows + i])
        for i, (source, target) in enumerate(
            ((q_hbm, q_ref), (new_hbm, new_ref), (offs_hbm, offs), (lens_hbm, lens))
        )
    ]
    copies = [pltpu.make_async_copy(cache.at[b], buf.at[b], sems.at[b]) for b in range(rows)]
    for copy in small + copies:
        copy.start()
    place = (lax.axis_index("y") * lax.axis_size("x") + lax.axis_index("x")) * lax.axis_size(
        "core"
    ) + lax.axis_index("core")
    shards = lax.axis_size("y") * lax.axis_size("x") * lax.axis_size("core")
    inv_root = 1.0 / HD**0.5
    lane = lanes(2 * group)
    first = (lane & 2) == 0
    low = lax.broadcasted_iota(jnp.int32, (2 * group, 1), 0) < group
    stat_lane = lanes(group)
    stats = [jnp.zeros((group, HD), F32), jnp.zeros((group, HD), F32)]
    for copy in small:
        copy.wait()
    for h in range(heads):
        q_by_row[pl.ds(h, rows, heads), :] = q_ref[:, h * HD : (h + 1) * HD].astype(F32)
    def products(b):
        limits, new_scores, new_values, queries = [], [], [], []
        for i in (b, b + 1):
            shard = lax.rem(place - offs[i] + shards, shards)
            limits.append((lens[i] - shard * slots) * 4)
            q = q_by_row[i * heads : (i + 1) * heads, :]
            new = new_ref[i].astype(F32)
            key_new = jnp.where(low, new[0:1, :HD], new[0:1, HD:])
            new_values.append(jnp.where(low, new[1:2, :HD], new[1:2, HD:]))
            score_new = jnp.sum(q * key_new, axis=1, keepdims=True) * inv_root
            new_scores.append(jnp.where(place == 0, score_new, -jnp.inf))
            queries.append(q)
        zero = jnp.zeros((heads, HD), F32)
        q = jnp.concatenate(
            [
                jnp.concatenate([queries[0], zero], axis=1),
                jnp.concatenate([zero, queries[1]], axis=1),
            ],
            axis=0,
        ).astype(BF16)
        copies[b].wait()
        copies[b + 1].wait()
        x = jnp.concatenate([buf[b], buf[b + 1]], axis=1)
        raw = lax.dot_general(q, x, (((1,), (1,)), ((), ())), preferred_element_type=F32)
        return x, raw, limits, new_scores, new_values

    ahead = products(0)
    for b in range(0, rows, 2):
        x, raw, limits, new_scores, new_values = ahead
        if b + 2 < rows:
            ahead = products(b + 2)
        left = jnp.where(low, limits[0], limits[1]) - lane
        left = jnp.where((lane & 1) == 0, left, -(1 << 30))
        scores = []
        for c in range(0, width, HD):
            part = raw[:, c : c + HD]
            head0 = jnp.concatenate([part[:group], part[heads : heads + group]], axis=0)
            head1 = jnp.concatenate([part[group:heads], part[heads + group :]], axis=0)
            scores.append(jnp.where(left > c, jnp.where(first, head0, head1), -jnp.inf))
        most = scores[0]
        for part in scores[1:]:
            most = jnp.maximum(most, part)
        tops = []
        for h, mine in enumerate((first, ~first)):
            top = jnp.max(jnp.where(mine, most, -jnp.inf), axis=1, keepdims=True) * inv_root
            new = jnp.concatenate([s[h * group : (h + 1) * group] for s in new_scores], axis=0)
            top = jnp.maximum(jnp.maximum(top, new), -1e30)
            tops.append(top.astype(BF16).astype(F32))
        shift = jnp.where(first, tops[0], tops[1]) * LOG2E
        total = jnp.zeros((2 * group, HD), F32)
        moved = []
        for part in scores:
            weight = jnp.exp2(part * (inv_root * LOG2E) - shift)
            total = total + weight
            moved.append(pltpu.roll(weight, 1, 1))
        moved = [[jnp.where(first, w, 0.0).astype(BF16), jnp.where(first, 0.0, w).astype(BF16)] for w in moved]
        lhs = [
            jnp.concatenate([pair[h][i * group : (i + 1) * group] for pair in moved], axis=1)
            for i in (0, 1)
            for h in (0, 1)
        ]
        summed = jnp.dot(jnp.concatenate(lhs, axis=0), x, preferred_element_type=F32)
        totals = [
            jnp.sum(jnp.where(mine, total, 0.0), axis=1, keepdims=True) for mine in (first, ~first)
        ]
        for i in (0, 1):
            for h in (0, 1):
                mine = slice(i * group, (i + 1) * group)
                theirs = slice(h * group, (h + 1) * group)
                top = tops[h][mine]
                weight_new = jnp.exp(new_scores[i][theirs] - top)
                value = summed[i * heads + h * group :][:group, i * HD : (i + 1) * HD]
                value = value + weight_new.astype(BF16).astype(F32) * new_values[i][theirs]
                block = value.astype(BF16)
                for dest in range(h, out_ref.shape[0], 2):
                    out_ref[dest, (b + i) * group : (b + i + 1) * group, :] = block
                stat = jnp.where(stat_lane == b + i, top, stats[h])
                stats[h] = jnp.where(stat_lane == HALF + b + i, totals[h][mine] + weight_new, stat)
    for h in (0, 1):
        for dest in range(h, out_ref.shape[0], 2):
            out_ref[dest, rows * group :, :] = stats[h].astype(BF16)


def join(parts, rows):
    group = parts[0].shape[0] // (rows + 1)
    stats = [part[rows * group :].astype(F32) for part in parts]
    top = stats[0]
    for stat in stats[1:]:
        top = jnp.maximum(top, stat)
    factors = [jnp.exp(stat - top) for stat in stats]
    total = sum(f * pltpu.roll(stat, HALF, 1) for f, stat in zip(factors, stats))
    sums = []
    for b in range(rows):
        mine = slice(b * group, (b + 1) * group)
        sums.append(sum(part[mine].astype(F32) * f[:, b : b + 1] for part, f in zip(parts, factors)))
    return sums, top, total


def combine_kernel(parts_ref, out_ref):
    parts = [parts_ref[i] for i in range(parts_ref.shape[0])]
    group = 16
    rows = parts_ref.shape[1] // group - 1
    sums, top, total = join(parts, rows)
    stats = jnp.where(lanes(group) < HALF, top, pltpu.roll(total, HALF, 1))
    block = jnp.concatenate(sums + [stats], axis=0).astype(BF16)
    out_ref[...] = jnp.broadcast_to(block[None], out_ref.shape)


def project_kernel(parts_ref, residual_ref, gain_ref, own_ref, theirs_ref, out_ref, attn):
    group = 16
    rows = parts_ref.shape[1] // group - 1
    sums, _, total = join([parts_ref[i] for i in range(parts_ref.shape[0])], rows)
    for b in range(rows):
        attn[b * group : (b + 1) * group, :] = sums[b] / total[:, b : b + 1]
    lhs = jnp.concatenate([attn[pl.ds(g, rows, group), :] for g in range(group)], axis=1).astype(BF16)
    mine = pl.ds(pl.multiple_of(lax.axis_index("core") * (group * HD), group * HD), group * HD)
    own = jnp.dot(lhs, own_ref[mine, :], preferred_element_type=F32)
    theirs = jnp.dot(lhs, theirs_ref[mine, :], preferred_element_type=F32)
    core0 = lax.axis_index("core") == 0
    total = jnp.concatenate([jnp.where(core0, own, theirs), jnp.where(core0, theirs, own)], axis=1)
    gain = jnp.broadcast_to(gain_ref[...].astype(F32).reshape(1, HD), (rows, HD))
    block = jnp.concatenate([total, residual_ref[...].astype(F32), gain], axis=1).astype(BF16)
    out_ref[...] = jnp.broadcast_to(block[None], out_ref.shape)


def stream_kernel(parts_ref, own_ref, out_ref):
    count, rows, width = parts_ref.shape
    width -= 2 * HD
    parts = parts_ref[...].astype(F32)
    total = parts[0, :, :width]
    for i in range(1, count):
        total = total + parts[i, :, :width]
    residual = jnp.concatenate([parts[i, :, width : width + HD] for i in range(count)], axis=1)
    wide = (total + residual).astype(BF16).astype(F32)
    gain = jnp.concatenate([parts[i, :, width + HD :] for i in range(count)], axis=1)
    squares = jnp.sum(wide * wide, axis=1, keepdims=True)
    high = squares.astype(BF16).astype(F32)
    tail = jnp.where(lanes(rows) < HALF, high, squares - high)
    block = jnp.concatenate([wide * gain, tail], axis=1).astype(BF16)
    out_ref[...] = jnp.broadcast_to(block[None], out_ref.shape)
    place = lax.axis_index("core") * lax.axis_size("head") + lax.axis_index("head")
    own = wide[:, :HD]
    for i in range(1, count):
        own = jnp.where(place == i, wide[:, i * HD : (i + 1) * HD], own)
    own_ref[...] = own.astype(BF16)


def gated_kernel(x_ref, own_ref, gate_ref, up_ref, stream_ref, out_ref):
    stream_ref[...] = own_ref[...]
    width = x_ref.shape[2] - HD
    tail = x_ref[:, :, width:].astype(F32)
    squares = jnp.sum(tail[:, :, 0:1] + tail[:, :, HALF : HALF + 1], axis=0)
    inv_norm = lax.rsqrt(squares / D + 1e-05)
    lhs = jnp.concatenate([x_ref[i, :, :width] for i in range(x_ref.shape[0])], axis=1)
    gate = jnp.dot(lhs, gate_ref[...], preferred_element_type=F32) * inv_norm
    up = jnp.dot(lhs, up_ref[...], preferred_element_type=F32) * inv_norm
    out_ref[...] = (gate / (1.0 + jnp.exp(-gate)) * up).astype(BF16)


def params(mib):
    return pltpu.CompilerParams(vmem_limit_bytes=mib * MIB)


def kernel_and_exchange():
    return pl.CostEstimate(flops=10**10, bytes_accessed=10**8, transcendentals=0)


def shards(
    queries,
    kv_cache,
    new_kv,
    offsets,
    lengths,
    residual,
    out_weight,
    norm_gain,
    gate_weight,
    up_weight,
):
    rows, slots = kv_cache.shape[:2]
    heads = queries.shape[1] // HD
    group = heads // 2
    ny, nx, nc, nz = (lax.axis_size(name) for name in ALL)
    width = out_weight.shape[1]
    message = rows * group + group
    cache = (
        kv_cache.reshape(rows, slots, 2, 2, HD)
        .transpose(0, 1, 3, 2, 4)
        .reshape(rows, slots * 4, HD)
    )
    parts = pl.pallas_call(
        attention_kernel,
        out_shape=pltpu.VMEM((nx * nc, message, HD), BF16),
        in_specs=[HBM] * 5,
        out_specs=VMEM,
        scratch_shapes=[
            pltpu.SMEM(offsets.shape, jnp.int32),
            pltpu.SMEM(lengths.shape, jnp.int32),
            pltpu.VMEM(queries.shape, BF16),
            pltpu.VMEM(new_kv.shape, BF16),
            pltpu.VMEM(cache.shape, BF16),
            pltpu.VMEM((rows * heads, HD), F32),
            pltpu.SemaphoreType.DMA((rows + 4,)),
        ],
        compiler_params=params(60),
        name="attention",
    )(offsets, lengths, queries, new_kv, cache)
    parts, moving = lax.optimization_barrier((parts, out_weight))
    theirs = lax.ppermute(moving, "core", [(0, 1), (1, 0)])
    parts = lax.all_to_all(parts, ("x", "core"), 0, 0, tiled=True)
    parts, theirs = lax.optimization_barrier((parts, theirs))
    parts = pl.pallas_call(
        combine_kernel,
        out_shape=jax.ShapeDtypeStruct((ny, message, HD), BF16),
        in_specs=[VMEM],
        out_specs=VMEM,
        compiler_params=params(8),
        cost_estimate=kernel_and_exchange(),
        name="combine",
    )(parts)
    parts = lax.all_to_all(parts, "y", 0, 0, tiled=True)
    partial = pl.pallas_call(
        project_kernel,
        out_shape=jax.ShapeDtypeStruct((nc * nz, rows, nc * width + 2 * HD), BF16),
        in_specs=[VMEM] * 5,
        out_specs=VMEM,
        scratch_shapes=[pltpu.VMEM((rows * group, HD), F32)],
        compiler_params=params(12),
        name="project",
    )(parts, residual, norm_gain, out_weight, theirs)
    partial = lax.all_to_all(partial, ("core", "head"), 0, 0, tiled=True)
    own, features = pl.pallas_call(
        stream_kernel,
        out_shape=(
            jax.ShapeDtypeStruct((rows, HD), BF16),
            jax.ShapeDtypeStruct((ny * nx, rows, nc * width + HD), BF16),
        ),
        in_specs=[VMEM],
        out_specs=(VMEM, VMEM),
        compiler_params=params(8),
        cost_estimate=kernel_and_exchange(),
        name="stream",
    )(partial)
    features = lax.all_to_all(features, ("y", "x"), 0, 0, tiled=True)
    return pl.pallas_call(
        gated_kernel,
        out_shape=(
            jax.ShapeDtypeStruct((rows, HD), BF16),
            jax.ShapeDtypeStruct((rows, gate_weight.shape[1]), BF16),
        ),
        in_specs=[VMEM] * 4,
        out_specs=(VMEM, VMEM),
        compiler_params=params(24),
        name="gated",
    )(features, own, gate_weight, up_weight)


def solution(mesh):
    split = Mesh(mesh.devices.reshape(4, 4, 2, 4), ALL)
    in_specs = (
        P(None, "head"),
        P(None, KV, None, "head"),
        P(None, None, "head"),
        P(),
        P(),
        P(None, ALL),
        P("head", KV),
        P(ALL),
        P(None, ALL),
        P(None, ALL),
    )
    out_specs = (P(None, ALL), P(None, ALL))
    return jax.shard_map(shards, mesh=split, in_specs=in_specs, out_specs=out_specs, check_vma=False)
```

profile of v0, /device:TPU:1, one launch (start us, length us, event | category | flops | bytes accessed | tf_op | source)
XLA Modules:
  0.0 55.8 jit_solution(14837039146188430739)
XLA Ops:
  0.6 4.1 %attention.1 = bf16[8,144,128]{2,1,0:T(8,128)(2,1)S(1)} custom-call(s32[8]{0:T(128)} %offs_hbm.1, s32[8]{0:T(128)} %lens_hbm.1, bf16[8,4096]{1,0:T(8,128)(2,1)} %q_hbm.1, bf16[8,2,256]{2,1,0:T(2,128)(2,1)} %new_hbm.1, bf16[8,2048,128]{2,1,0:T(8,128)(2,1)} %bitcast.9), custom_call_target="tpu_custom_call" | custom-call | tf_op jit(solution)/shard_map/attention/pallas_call | solution.py:246
  4.7 1.5 %collective-permute-start = (bf16[4096,512]{1,0:T(8,128)(2,1)}, bf16[4096,512]{1,0:T(8,128)(2,1)S(1)}, u32[]{:S(2)}, u32[]{:S(2)}) collective-permute-start(bf16[4096,512]{1,0:T(8,128)(2,1)} %own_ref.1), channel_id=1, source_target_pairs={{0,4},{4,0},{1,5},{5,1},{2,6},{6,2},{3,7},{7,3},{8,12},{12,8},{9,1... | collective-permute-start | bytes 12582920 | tf_op jit(solution)/shard_map/ppermute | solution.py:264
  6.2 11.6 %all_to_all.20.parts_ref = bf16[8,144,128]{2,1,0:T(8,128)(2,1)S(1)} all-to-all(bf16[8,144,128]{2,1,0:T(8,128)(2,1)S(1)} %attention.1), channel_id=1, replica_groups=mesh['y'=4,'x'=4,'core'=2,'head'=4] {'x','core'}, dimensions={0} | all-to-all | bytes 589824 | tf_op jit(solution)/shard_map/all_to_all | solution.py:265
  17.8 0.0 copy-start
  17.8 0.0 copy-start.1
  17.8 0.0 copy-start.2
  17.8 0.0 collective-permute-done.theirs_ref
  17.8 0.2 combine.1
  18.1 9.2 %all_to_all.21.parts_ref = bf16[4,144,128]{2,1,0:T(8,128)(2,1)S(1)} all-to-all(bf16[4,144,128]{2,1,0:T(8,128)(2,1)S(1)} %combine.1), channel_id=1, replica_groups=mesh['y'=4,'x'=4,'core'=2,'head'=4] {'y'}, dimensions={0} | all-to-all | bytes 294912 | tf_op jit(solution)/shard_map/all_to_all | solution.py:276
  27.2 0.0 copy-done
  27.2 0.0 copy-done.1
  27.2 0.0 copy-done.2
  27.3 0.8 %project.1 = bf16[8,8,1280]{2,1,0:T(8,128)(2,1)S(1)} custom-call(bf16[4,144,128]{2,1,0:T(8,128)(2,1)S(1)} %all_to_all.21.parts_ref, bf16[8,128]{1,0:T(8,128)(2,1)S(1)} %copy-done.1, bf16[128]{0:T(256)(128)(2,1)S(1)} %copy-done.2, bf16[4096,512]{1,0:T(8,128)(2,1)S(1)} %copy-done, bf16[4096,512]{1,0:T(8,128)(2,1)S(1)} %collective-permute-done.theirs_ref), custom_call_target="tpu_custom_call" | custom-call | tf_op jit(solution)/shard_map/project/pallas_call | solution.py:277
  28.1 0.0 slice-start
  28.1 0.0 slice-start.2
  28.1 12.9 %all_to_all.22.parts_ref = bf16[8,8,1280]{2,1,0:T(8,128)(2,1)S(1)} all-to-all(bf16[8,8,1280]{2,1,0:T(8,128)(2,1)S(1)} %project.1), channel_id=1, replica_groups=mesh['y'=4,'x'=4,'core'=2,'head'=4] {'core','head'}, dimensions={0} | all-to-all | bytes 327680 | tf_op jit(solution)/shard_map/all_to_all | solution.py:286
  41.0 0.0 slice-start.1
  41.0 0.0 slice-start.3
  41.0 0.1 stream.1
  41.1 11.8 %all_to_all.23.x_ref = bf16[16,8,1152]{2,1,0:T(8,128)(2,1)S(1)} all-to-all(bf16[16,8,1152]{2,1,0:T(8,128)(2,1)S(1)} %get-tuple-element.12), channel_id=1, replica_groups=mesh['y'=4,'x'=4,'core'=2,'head'=4] {'y','x'}, dimensions={0} | all-to-all | bytes 589824 | tf_op jit(solution)/shard_map/all_to_all | solution.py:299
  52.9 0.0 slice-done
  52.9 0.0 slice-done.2
  52.9 0.0 slice-done.1
  52.9 0.0 slice-done.3
  52.9 2.9 %gated.1 = (bf16[8,128]{1,0:T(8,128)(2,1)}, bf16[8,256]{1,0:T(8,128)(2,1)}) custom-call(bf16[16,8,1152]{2,1,0:T(8,128)(2,1)S(1)} %all_to_all.23.x_ref, bf16[8,128]{1,0:T(8,128)(2,1)S(1)} %get-tuple-element.13.own_ref, bf16[16384,256]{1,0:T(8,128)(2,1)S(1)} %bitcast.6, bf16[16384,256]{1,0:T(8,128)(2,1)S(1)} %bitcast.8), custom_call_target="tpu_custom_call" | custom-call | tf_op jit(solution)/shard_map/gated/pallas_call | solution.py:300
  (2 shorter events, 0.0 us)
Async XLA Ops:
  4.7 13.1 %collective-permute-start = (bf16[4096,512]{1,0:T(8,128)(2,1)}, bf16[4096,512]{1,0:T(8,128)(2,1)S(1)}, u32[]{:S(2)}, u32[]{:S(2)}) collective-permute-start(bf16[4096,512]{1,0:T(8,128)(2,1)} %own_ref.1), channel_id=1, source_target_pairs={{0,4},{4,0},{1,5},{5,1},{2,6},{6,2},{3,7},{7,3},{8,12},{12,8},{9,1... | collective-permute-start | bytes 12582920 | tf_op jit(solution)/shard_map/ppermute | solution.py:264
  17.8 9.4 %copy-start = (bf16[4096,512]{1,0:T(8,128)(2,1)S(1)}, bf16[4096,512]{1,0:T(8,128)(2,1)}, u32[]{:S(2)}) copy-start(bf16[4096,512]{1,0:T(8,128)(2,1)} %own_ref.1) | copy-start | bytes 12582916
  17.8 9.4 %copy-start.1 = (bf16[8,128]{1,0:T(8,128)(2,1)S(1)}, bf16[8,128]{1,0:T(8,128)(2,1)}, u32[]{:S(2)}) copy-start(bf16[8,128]{1,0:T(8,128)(2,1)} %residual_ref.1) | copy-start | bytes 6148
  17.8 9.4 %copy-start.2 = (bf16[128]{0:T(256)(128)(2,1)S(1)}, bf16[128]{0:T(256)(128)(2,1)}, u32[]{:S(2)}) copy-start(bf16[128]{0:T(256)(128)(2,1)} %gain_ref.1) | copy-start | bytes 772
  28.1 24.8 %slice-start = ((s8[8388608]{0:T(1024)(128)(4,1)}), s8[4194304]{0:T(1024)(128)(4,1)S(1)}, s32[]{:S(2)}) async-start(s8[8388608]{0:T(1024)(128)(4,1)} %bitcast.5), calls=%async_computation.4 | async-start | bytes 8388608
  28.1 24.8 %slice-start.2 = ((s8[8388608]{0:T(1024)(128)(4,1)}), s8[4194304]{0:T(1024)(128)(4,1)S(1)}, s32[]{:S(2)}) async-start(s8[8388608]{0:T(1024)(128)(4,1)} %bitcast.7), calls=%async_computation.6 | async-start | bytes 8388608
  41.0 11.9 %slice-start.1 = ((s8[8388608]{0:T(1024)(128)(4,1)}), s8[4194304]{0:T(1024)(128)(4,1)S(1)}, s32[]{:S(2)}) async-start(s8[8388608]{0:T(1024)(128)(4,1)} %bitcast.5), calls=%async_computation.5 | async-start | bytes 8388608
  41.0 11.9 %slice-start.3 = ((s8[8388608]{0:T(1024)(128)(4,1)}), s8[4194304]{0:T(1024)(128)(4,1)S(1)}, s32[]{:S(2)}) async-start(s8[8388608]{0:T(1024)(128)(4,1)} %bitcast.7), calls=%async_computation.7 | async-start | bytes 8388608
where the time goes:
time: 56.1 us; the launch traced here: 55.8 us
  blocking collectives  45.5 us (81%)
  Pallas kernels  8.13 us (14%)
  starting transfers between devices  1.5 us (3%)
  between operations  0.71 us (1%)
    all_to_all x1, blocking collectives, shards(): partial = lax.all_to_all(partial, ('core', 'head'), 0, 0, tiled=True)  12.9 us
    all_to_all x1, blocking collectives, shards(): features = lax.all_to_all(features, ('y', 'x'), 0, 0, tiled=True)  11.8 us
    all_to_all x1, blocking collectives, shards(): parts = lax.all_to_all(parts, ('x', 'core'), 0, 0, tiled=True)  11.6 us
    all_to_all x1, blocking collectives, shards(): parts = lax.all_to_all(parts, 'y', 0, 0, tiled=True)  9.16 us
    pallas_call x1, Pallas kernels, shards(): pl.pallas_call(attention_kernel, out_shape=pltpu.VMEM((nx * nc, message,...  4.08 us
    pallas_call x1, Pallas kernels, shards(): pl.pallas_call(gated_kernel, out_shape=(jax.ShapeDtypeStruct((rows, HD),...  2.88 us
    ppermute x1, starting transfers between devices, shards(): theirs = lax.ppermute(moving, 'core', [(0, 1), (1, 0)])  1.5 us
  transfers between devices with their start and end apart: 1, of which 0 were waited for; matrix products, arithmetic and copies ran while one was open for 0% of the time, Pallas kernels for 0%

commit v1 on v0

--- a/solution.py
+++ b/solution.py
@@ -171,23 +171,28 @@
     mine = pl.ds(pl.multiple_of(lax.axis_index("core") * (group * HD), group * HD), group * HD)
     own = jnp.dot(lhs, own_ref[mine, :], preferred_element_type=F32)
     theirs = jnp.dot(lhs, theirs_ref[mine, :], preferred_element_type=F32)
-    core0 = lax.axis_index("core") == 0
-    total = jnp.concatenate([jnp.where(core0, own, theirs), jnp.where(core0, theirs, own)], axis=1)
+    core = lax.axis_index("core")
+    total = jnp.concatenate(
+        [jnp.where(core == 0, own, theirs), jnp.where(core == 0, theirs, own)], axis=1
+    )
     gain = jnp.broadcast_to(gain_ref[...].astype(F32).reshape(1, HD), (rows, HD))
-    block = jnp.concatenate([total, residual_ref[...].astype(F32), gain], axis=1).astype(BF16)
+    place = core * lax.axis_size("head") + lax.axis_index("head")
+    residual = jnp.concatenate([residual_ref[...].astype(F32)] * (total.shape[1] // HD), axis=1)
+    column = lax.broadcasted_iota(jnp.int32, total.shape, 1)
+    mine = (column >= place * HD) & (column < place * HD + HD)
+    block = jnp.concatenate([total + jnp.where(mine, residual, 0.0), gain], axis=1).astype(BF16)
     out_ref[...] = jnp.broadcast_to(block[None], out_ref.shape)
 
 
 def stream_kernel(parts_ref, own_ref, out_ref):
     count, rows, width = parts_ref.shape
-    width -= 2 * HD
+    width -= HD
     parts = parts_ref[...].astype(F32)
     total = parts[0, :, :width]
     for i in range(1, count):
         total = total + parts[i, :, :width]
-    residual = jnp.concatenate([parts[i, :, width : width + HD] for i in range(count)], axis=1)
-    wide = (total + residual).astype(BF16).astype(F32)
-    gain = jnp.concatenate([parts[i, :, width + HD :] for i in range(count)], axis=1)
+    wide = total.astype(BF16).astype(F32)
+    gain = jnp.concatenate([parts[i, :, width:] for i in range(count)], axis=1)
     squares = jnp.sum(wide * wide, axis=1, keepdims=True)
     high = squares.astype(BF16).astype(F32)
     tail = jnp.where(lanes(rows) < HALF, high, squares - high)
@@ -276,7 +281,7 @@
     parts = lax.all_to_all(parts, "y", 0, 0, tiled=True)
     partial = pl.pallas_call(
         project_kernel,
-        out_shape=jax.ShapeDtypeStruct((nc * nz, rows, nc * width + 2 * HD), BF16),
+        out_shape=jax.ShapeDtypeStruct((nc * nz, rows, nc * width + HD), BF16),
         in_specs=[VMEM] * 5,
         out_specs=VMEM,
         scratch_shapes=[pltpu.VMEM((rows * group, HD), F32)],

time: 56.1 us -> 55.9 us (level)
  no operation moved by 1% of the time
where the time goes in v1:
time: 55.9 us; the launch traced here: 55.7 us
  blocking collectives  45.3 us (81%)
  Pallas kernels  8.12 us (15%)
  starting transfers between devices  1.5 us (3%)
  between operations  0.71 us (1%)
    all_to_all x1, blocking collectives, shards(): partial = lax.all_to_all(partial, ('core', 'head'), 0, 0, tiled=True)  12.7 us
    all_to_all x1, blocking collectives, shards(): features = lax.all_to_all(features, ('y', 'x'), 0, 0, tiled=True)  11.9 us
    all_to_all x1, blocking collectives, shards(): parts = lax.all_to_all(parts, ('x', 'core'), 0, 0, tiled=True)  11.6 us
    all_to_all x1, blocking collectives, shards(): parts = lax.all_to_all(parts, 'y', 0, 0, tiled=True)  9.16 us
    pallas_call x1, Pallas kernels, shards(): pl.pallas_call(attention_kernel, out_shape=pltpu.VMEM((nx * nc, message,...  4.08 us
    pallas_call x1, Pallas kernels, shards(): pl.pallas_call(gated_kernel, out_shape=(jax.ShapeDtypeStruct((rows, HD),...  2.88 us
    ppermute x1, starting transfers between devices, shards(): theirs = lax.ppermute(moving, 'core', [(0, 1), (1, 0)])  1.5 us
  transfers between devices with their start and end apart: 1, of which 0 were waited for; matrix products, arithmetic and copies ran while one was open for 0% of the time, Pallas kernels for 0%

profile of v1, /device:TPU:1, one launch (start us, length us, event | category | flops | bytes accessed | tf_op | source)
XLA Modules:
  0.0 55.7 jit_solution(11633322245700731797)
XLA Ops:
  0.6 4.1 %attention.1 = bf16[8,144,128]{2,1,0:T(8,128)(2,1)S(1)} custom-call(s32[8]{0:T(128)} %offs_hbm.1, s32[8]{0:T(128)} %lens_hbm.1, bf16[8,4096]{1,0:T(8,128)(2,1)} %q_hbm.1, bf16[8,2,256]{2,1,0:T(2,128)(2,1)} %new_hbm.1, bf16[8,2048,128]{2,1,0:T(8,128)(2,1)} %bitcast.9), custom_call_target="tpu_custom_call" | custom-call | tf_op jit(solution)/shard_map/attention/pallas_call | solution.py:251
  4.7 1.5 %collective-permute-start = (bf16[4096,512]{1,0:T(8,128)(2,1)}, bf16[4096,512]{1,0:T(8,128)(2,1)S(1)}, u32[]{:S(2)}, u32[]{:S(2)}) collective-permute-start(bf16[4096,512]{1,0:T(8,128)(2,1)} %own_ref.1), channel_id=1, source_target_pairs={{0,4},{4,0},{1,5},{5,1},{2,6},{6,2},{3,7},{7,3},{8,12},{12,8},{9,1... | collective-permute-start | bytes 12582920 | tf_op jit(solution)/shard_map/ppermute | solution.py:269
  6.2 11.6 %all_to_all.20.parts_ref = bf16[8,144,128]{2,1,0:T(8,128)(2,1)S(1)} all-to-all(bf16[8,144,128]{2,1,0:T(8,128)(2,1)S(1)} %attention.1), channel_id=1, replica_groups=mesh['y'=4,'x'=4,'core'=2,'head'=4] {'x','core'}, dimensions={0} | all-to-all | bytes 589824 | tf_op jit(solution)/shard_map/all_to_all | solution.py:270
  17.8 0.0 copy-start
  17.8 0.0 copy-start.1
  17.8 0.0 copy-start.2
  17.8 0.0 collective-permute-done.theirs_ref
  17.8 0.2 combine.1
  18.1 9.2 %all_to_all.21.parts_ref = bf16[4,144,128]{2,1,0:T(8,128)(2,1)S(1)} all-to-all(bf16[4,144,128]{2,1,0:T(8,128)(2,1)S(1)} %combine.1), channel_id=1, replica_groups=mesh['y'=4,'x'=4,'core'=2,'head'=4] {'y'}, dimensions={0} | all-to-all | bytes 294912 | tf_op jit(solution)/shard_map/all_to_all | solution.py:281
  27.2 0.0 copy-done
  27.2 0.0 copy-done.1
  27.2 0.0 copy-done.2
  27.3 0.8 %project.1 = bf16[8,8,1152]{2,1,0:T(8,128)(2,1)S(1)} custom-call(bf16[4,144,128]{2,1,0:T(8,128)(2,1)S(1)} %all_to_all.21.parts_ref, bf16[8,128]{1,0:T(8,128)(2,1)S(1)} %copy-done.1, bf16[128]{0:T(256)(128)(2,1)S(1)} %copy-done.2, bf16[4096,512]{1,0:T(8,128)(2,1)S(1)} %copy-done, bf16[4096,512]{1,0:T(8,128)(2,1)S(1)} %collective-permute-done.theirs_ref), custom_call_target="tpu_custom_call" | custom-call | tf_op jit(solution)/shard_map/project/pallas_call | solution.py:282
  28.1 0.0 slice-start
  28.1 0.0 slice-start.2
  28.1 12.7 %all_to_all.22.parts_ref = bf16[8,8,1152]{2,1,0:T(8,128)(2,1)S(1)} all-to-all(bf16[8,8,1152]{2,1,0:T(8,128)(2,1)S(1)} %project.1), channel_id=1, replica_groups=mesh['y'=4,'x'=4,'core'=2,'head'=4] {'core','head'}, dimensions={0} | all-to-all | bytes 294912 | tf_op jit(solution)/shard_map/all_to_all | solution.py:291
  40.8 0.0 slice-start.1
  40.8 0.0 slice-start.3
  40.8 0.1 stream.1
  40.9 11.9 %all_to_all.23.x_ref = bf16[16,8,1152]{2,1,0:T(8,128)(2,1)S(1)} all-to-all(bf16[16,8,1152]{2,1,0:T(8,128)(2,1)S(1)} %get-tuple-element.12), channel_id=1, replica_groups=mesh['y'=4,'x'=4,'core'=2,'head'=4] {'y','x'}, dimensions={0} | all-to-all | bytes 589824 | tf_op jit(solution)/shard_map/all_to_all | solution.py:304
  52.8 0.0 slice-done
  52.8 0.0 slice-done.2
  52.8 0.0 slice-done.1
  52.8 0.0 slice-done.3
  52.8 2.9 %gated.1 = (bf16[8,128]{1,0:T(8,128)(2,1)}, bf16[8,256]{1,0:T(8,128)(2,1)}) custom-call(bf16[16,8,1152]{2,1,0:T(8,128)(2,1)S(1)} %all_to_all.23.x_ref, bf16[8,128]{1,0:T(8,128)(2,1)S(1)} %get-tuple-element.13.own_ref, bf16[16384,256]{1,0:T(8,128)(2,1)S(1)} %bitcast.6, bf16[16384,256]{1,0:T(8,128)(2,1)S(1)} %bitcast.8), custom_call_target="tpu_custom_call" | custom-call | tf_op jit(solution)/shard_map/gated/pallas_call | solution.py:305
  (2 shorter events, 0.0 us)
Async XLA Ops:
  4.7 13.1 %collective-permute-start = (bf16[4096,512]{1,0:T(8,128)(2,1)}, bf16[4096,512]{1,0:T(8,128)(2,1)S(1)}, u32[]{:S(2)}, u32[]{:S(2)}) collective-permute-start(bf16[4096,512]{1,0:T(8,128)(2,1)} %own_ref.1), channel_id=1, source_target_pairs={{0,4},{4,0},{1,5},{5,1},{2,6},{6,2},{3,7},{7,3},{8,12},{12,8},{9,1... | collective-permute-start | bytes 12582920 | tf_op jit(solution)/shard_map/ppermute | solution.py:269
  17.8 9.4 %copy-start = (bf16[4096,512]{1,0:T(8,128)(2,1)S(1)}, bf16[4096,512]{1,0:T(8,128)(2,1)}, u32[]{:S(2)}) copy-start(bf16[4096,512]{1,0:T(8,128)(2,1)} %own_ref.1) | copy-start | bytes 12582916
  17.8 9.4 %copy-start.1 = (bf16[8,128]{1,0:T(8,128)(2,1)S(1)}, bf16[8,128]{1,0:T(8,128)(2,1)}, u32[]{:S(2)}) copy-start(bf16[8,128]{1,0:T(8,128)(2,1)} %residual_ref.1) | copy-start | bytes 6148
  17.8 9.4 %copy-start.2 = (bf16[128]{0:T(256)(128)(2,1)S(1)}, bf16[128]{0:T(256)(128)(2,1)}, u32[]{:S(2)}) copy-start(bf16[128]{0:T(256)(128)(2,1)} %gain_ref.1) | copy-start | bytes 772
  28.1 24.7 %slice-start = ((s8[8388608]{0:T(1024)(128)(4,1)}), s8[4194304]{0:T(1024)(128)(4,1)S(1)}, s32[]{:S(2)}) async-start(s8[8388608]{0:T(1024)(128)(4,1)} %bitcast.5), calls=%async_computation.4 | async-start | bytes 8388608
  28.1 24.7 %slice-start.2 = ((s8[8388608]{0:T(1024)(128)(4,1)}), s8[4194304]{0:T(1024)(128)(4,1)S(1)}, s32[]{:S(2)}) async-start(s8[8388608]{0:T(1024)(128)(4,1)} %bitcast.7), calls=%async_computation.6 | async-start | bytes 8388608
  40.8 12.0 %slice-start.1 = ((s8[8388608]{0:T(1024)(128)(4,1)}), s8[4194304]{0:T(1024)(128)(4,1)S(1)}, s32[]{:S(2)}) async-start(s8[8388608]{0:T(1024)(128)(4,1)} %bitcast.5), calls=%async_computation.5 | async-start | bytes 8388608
  40.8 12.0 %slice-start.3 = ((s8[8388608]{0:T(1024)(128)(4,1)}), s8[4194304]{0:T(1024)(128)(4,1)S(1)}, s32[]{:S(2)}) async-start(s8[8388608]{0:T(1024)(128)(4,1)} %bitcast.7), calls=%async_computation.7 | async-start | bytes 8388608
